TPU v7x, 32 devices: a whole 2x2x4 slice. The times are simulated.
32 devices in a mesh: seq: 8 (over z, y), head: 4 (over x, core).
Axes of the slice: x: 2, y: 2, z: 4, core: 2. Of those that a mesh axis runs over, the one named last changes fastest.
Arguments:
- queries: bfloat16 [1024, 4096], P('seq', 'head')
- keys: bfloat16 [1024, 1024], P('seq', 'head')
- values: bfloat16 [1024, 1024], P('seq', 'head'), may hold values from -6 to 6
- out_weight: bfloat16 [4096, 4096], P('head'), may hold values from -0.09375 to 0.09375
- windows: int32 [32], replicated, may hold values from 128 to 512, as said below
- seg_lengths: int32 [64], replicated, may hold values from 1 to 48, 1024 in all
- lang_ids: int32 [64], replicated, may hold values from 0 to 7
Outputs:
- centered: bfloat16 [1024, 4096], P('seq', 'head')
- pooled: float32 [64, 4096], P(None, 'head')
Inputs may be any that keep to these rules, and one draw needn't show every extreme that they name: `windows`: each head's window; some head has exactly 512. `seg_lengths`: the spans tile the document; the longest is exactly 48.
All inputs are finite; a program needn't handle non-finite values.
Results may differ from a plain program's by a relative error of at most 0.014.
Values may be sent and summed in bfloat16 or wider, within the bound.
A program may use at most 64 MiB of HBM per device.

v0:
```python
import jax
import jax.numpy as jnp
from jax import lax
from jax.sharding import PartitionSpec as P

HD = 128
NLANG = 8


def shifted(block, axis, distance):
    devices = range(lax.axis_size(axis))
    route = [(i - distance, i) for i in devices if i - distance in devices]
    return lax.ppermute(block, axis, route)


def on_device(queries, keys, values, out_weight, windows, seg_lengths, lang_ids):
    tok = queries.shape[0]
    q_heads = queries.shape[1] // HD
    kv_heads = keys.shape[1] // HD
    group = q_heads // kv_heads
    seq_count = lax.axis_size("seq")
    reach = min(16, seq_count // 2)
    total_len = tok * seq_count
    seq_me = lax.axis_index("seq")
    head_me = lax.axis_index("head")
    query_pos = seq_me * tok + jnp.arange(tok, dtype=jnp.int32)
    my_windows = lax.dynamic_slice_in_dim(windows, head_me * q_heads, q_heads).reshape(
        kv_heads, group
    )
    query_grid = queries.reshape(tok, kv_heads, group, HD)
    kv_cols = kv_heads * HD
    paired = jnp.concatenate([keys, values], axis=1)
    local_rows = jnp.arange(tok, dtype=jnp.int32)

    def absorb(state, block, key_pos):
        count = block.shape[0]
        key_block = block[:, :kv_cols].reshape(count, kv_heads, HD)
        value_block = block[:, kv_cols:].reshape(count, kv_heads, HD)
        scores = jnp.einsum(
            "tkgd,nkd->kgtn", query_grid, key_block, preferred_element_type=jnp.float32
        ) * HD ** (-0.5)
        distance = jnp.abs(query_pos[:, None] - key_pos[None, :])
        inside = (key_pos >= 0) & (key_pos < total_len)
        allowed = (distance[None, None] <= my_windows[:, :, None, None]) & inside[
            None, None, None, :
        ]
        scores = jnp.where(allowed, scores, jnp.float32(-1e30))
        top_old, total_old, accum = state
        top_new = jnp.maximum(top_old, jnp.max(scores, axis=-1))
        rescale = jnp.exp(top_old - top_new)
        probs = jnp.where(allowed, jnp.exp(scores - top_new[..., None]), jnp.float32(0.0))
        total_new = total_old * rescale + jnp.sum(probs, axis=-1)
        weighted = jnp.einsum(
            "kgtn,nkd->kgtd",
            probs.astype(jnp.bfloat16),
            value_block,
            preferred_element_type=jnp.float32,
        )
        return (top_new, total_new, accum * rescale[..., None] + weighted)

    state = (
        jnp.full((kv_heads, group, tok), -1e30, jnp.float32),
        jnp.zeros((kv_heads, group, tok), jnp.float32),
        jnp.zeros((kv_heads, group, tok, HD), jnp.float32),
    )
    state = absorb(state, paired, query_pos)
    factor = 4
    for first in range(1, reach + 1, factor):
        pieces = []
        places = []
        for step in range(first, first + factor):
            pieces.append(shifted(paired, "seq", step))
            places.append((seq_me - step) * tok + local_rows)
            pieces.append(shifted(paired, "seq", -step))
            places.append((seq_me + step) * tok + local_rows)
        state = absorb(state, jnp.concatenate(pieces, axis=0), jnp.concatenate(places, axis=0))
    top_final, total_final, accum = state
    mixed = accum / total_final[..., None]
    attn = mixed.transpose(2, 0, 1, 3).reshape(tok, q_heads * HD).astype(jnp.bfloat16)
    partial_sums = jnp.dot(attn, out_weight, preferred_element_type=jnp.float32)
    tokens = lax.psum_scatter(
        partial_sums.astype(jnp.bfloat16), "head", scatter_dimension=1, tiled=True
    ).astype(jnp.float32)
    ends = jnp.cumsum(seg_lengths)
    starts = ends - seg_lengths
    seg_hot = (
        (query_pos[:, None] >= starts[None, :]) & (query_pos[:, None] < ends[None, :])
    ).astype(jnp.float32)
    span_part = jnp.dot(seg_hot.T, tokens, precision=lax.Precision.HIGHEST)
    span_sum = lax.psum(span_part, "seq")
    lang_hot = (lang_ids[:, None] == jnp.arange(NLANG, dtype=jnp.int32)[None, :]).astype(
        jnp.float32
    )
    lang_sum = jnp.dot(lang_hot.T, span_sum, precision=lax.Precision.HIGHEST)
    lang_count = jnp.sum(lang_hot * seg_lengths.astype(jnp.float32)[:, None], axis=0)
    lang_mean = lang_sum / jnp.maximum(lang_count, 1.0)[:, None]
    seg_center = jnp.dot(lang_hot, lang_mean, precision=lax.Precision.HIGHEST)
    centered = (tokens - jnp.dot(seg_hot, seg_center, precision=lax.Precision.HIGHEST)).astype(
        jnp.bfloat16
    )
    pooled = span_sum / seg_lengths.astype(jnp.float32)[:, None] - seg_center
    return (centered, pooled)


def solution(mesh):
    in_specs = (
        P("seq", "head"),
        P("seq", "head"),
        P("seq", "head"),
        P("head", None),
        P(),
        P(),
        P(),
    )
    out_specs = (P("seq", "head"), P(None, "head"))
    return jax.shard_map(
        on_device, mesh=mesh, in_specs=in_specs, out_specs=out_specs, check_vma=False
    )
```

profile of v0, /device:TPU:0, one launch (start us, length us, event | category | flops | bytes accessed | tf_op | source)
XLA Modules:
  0.0 166.1 jit_solution(14637802232511220271)
XLA Ops:
  7.2 0.9 copy.45
  8.2 1.0 copy.31
  9.1 4.9 %collective-permute-start = (bf16[128,512]{0,1:T(8,128)(2,1)S(1)}, bf16[128,512]{0,1:T(8,128)(2,1)S(1)}, u32[]{:S(2)}, u32[]{:S(2)}) collective-permute-start(bf16[128,512]{0,1:T(8,128)(2,1)S(1)} %pad_maximum_fusion), channel_id=1, source_target_pairs={{0,4},{4,8},{8,12},{12,16},{16,20},{20,24},{24,28},{1,5},{5,9},{9,... | collective-permute-start | bytes 393224 | tf_op jit(solution)/shard_map/ppermute | solution.py:13
  14.0 1.3 collective-permute-start.1
  15.3 5.5 %collective-permute-start.2 = (bf16[128,512]{0,1:T(8,128)(2,1)S(1)}, bf16[128,512]{0,1:T(8,128)(2,1)S(1)}, u32[]{:S(2)}, u32[]{:S(2)}) collective-permute-start(bf16[128,512]{0,1:T(8,128)(2,1)S(1)} %pad_maximum_fusion), channel_id=1, source_target_pairs={{0,8},{4,12},{8,16},{12,20},{16,24},{20,28},{1,9},{5,13},{9,17},{1... | collective-permute-start | bytes 393224 | tf_op jit(solution)/shard_map/ppermute | solution.py:13
  20.8 1.3 collective-permute-start.3
  22.1 4.6 %collective-permute-start.4 = (bf16[128,512]{0,1:T(8,128)(2,1)S(1)}, bf16[128,512]{0,1:T(8,128)(2,1)S(1)}, u32[]{:S(2)}, u32[]{:S(2)}) collective-permute-start(bf16[128,512]{0,1:T(8,128)(2,1)S(1)} %pad_maximum_fusion), channel_id=1, source_target_pairs={{0,12},{4,16},{8,20},{12,24},{16,28},{1,13},{5,17},{9,21},{13,25},... | collective-permute-start | bytes 393224 | tf_op jit(solution)/shard_map/ppermute | solution.py:13
  26.8 0.9 reshape.236
  27.9 0.2 subtract_abs_fusion
  28.1 0.7 dynamic_slice.3
  28.9 1.1 reshape.237
  30.0 0.3 fusion.55
  30.3 1.3 collective-permute-start.5
  31.7 7.3 %collective-permute-start.6 = (bf16[128,512]{0,1:T(8,128)(2,1)S(1)}, bf16[128,512]{0,1:T(8,128)(2,1)S(1)}, u32[]{:S(2)}, u32[]{:S(2)}) collective-permute-start(bf16[128,512]{0,1:T(8,128)(2,1)S(1)} %pad_maximum_fusion), channel_id=1, source_target_pairs={{0,16},{4,20},{8,24},{12,28},{1,17},{5,21},{9,25},{13,29},{2,18},{... | collective-permute-start | bytes 393224 | tf_op jit(solution)/shard_map/ppermute | solution.py:13
  39.0 1.3 collective-permute-start.7
  40.5 0.9 collective-permute-done.6
  41.5 6.7 %collective-permute-done.7 = bf16[128,512]{0,1:T(8,128)(2,1)S(1)} collective-permute-done((bf16[128,512]{0,1:T(8,128)(2,1)S(1)}, bf16[128,512]{0,1:T(8,128)(2,1)S(1)}, u32[]{:S(2)}, u32[]{:S(2)}) %collective-permute-start.7) | collective-permute-done | bytes 131104 | tf_op jit(solution)/shard_map/ppermute | solution.py:13
  48.3 1.5 fusion
  49.8 0.2 fusion.21
  50.0 2.0 %fusion.20 = f32[2,4,128]{2,1,0:T(4,128)S(1)} fusion(f32[2,4,128]{2,1,0:T(4,128)S(1)} %get-tuple-element.8, f32[2,1024,128,4]{2,1,3,0:T(8,128)S(1)} %get-tuple-element.14, pred[1024]{0:T(1024)(128)(4,1)S(1)} %compare_and_fusion.5, s32[2,4]{1,0:T(2,128)S(1)} %le.29, s32[128,1024]{0,1:T(8,128)S(1)} %subtract_abs_fusion), kind=kLoop, calls=%fused_computation.20 | loop fusion | flops 7339008 | bytes 4727840 | tf_op jit(solution)/shard_map/reduce_sum | solution.py:52
  52.1 0.3 fusion.4
  52.4 1.6 fusion.16
  54.0 0.6 slice-done.1
  54.6 2.3 %convolution_convert_fusion = bf16[128,4096]{1,0:T(8,128)(2,1)} fusion(bf16[128,1024]{0,1:T(8,128)(2,1)S(1)} %bitcast.79, bf16[1024,4096]{1,0:T(8,128)(2,1)S(1)} %bitcast.78), kind=kOutput, calls=%fused_computation | convolution fusion | flops 1074266112 | bytes 9699328 | tf_op jit(solution)/shard_map/dot_general | solution.py:80
  57.1 0.1 reduce
  57.3 22.0 %reduce-scatter.2.cloned.1.call-done = bf16[128,1024]{1,0:T(8,128)(2,1)} async-done(((bf16[128,4096]{1,0:T(8,128)(2,1)}), bf16[128,1024]{1,0:T(8,128)(2,1)}) %reduce-scatter.2.cloned.1.call-update) | async-done | bytes 262160 | tf_op jit(solution)/shard_map/reduce_scatter | solution.py:81
  79.2 1.9 %fusion.33 = f32[64,1024]{1,0:T(8,128)} fusion(bf16[128,1024]{1,0:T(8,128)(2,1)} %reduce-scatter.2.cloned.1.call-done, s32[64]{0:T(128)S(1)} %reduce, s32[64]{0:T(128)S(1)} %get-tuple-element.10, s32[128]{0:T(128)S(1)} %get-tuple-element.18), kind=kOutput, calls=%fused_computation.39 | convolution fusion | flops 16801792 | bytes 525312 | tf_op jit(solution)/shard_map/dot_general | solution.py:89
  81.2 0.1 select_reduce_fusion
  81.3 72.8 %all-reduce.2.cloned.1.call-done = f32[64,1024]{1,0:T(8,128)} async-done(((f32[64,1024]{1,0:T(8,128)}), f32[64,1024]{1,0:T(8,128)}) %all-reduce.2.cloned.1.call-update) | async-done | bytes 262160 | tf_op jit(solution)/shard_map/psum | solution.py:90
  154.1 1.2 convolution_divide_fusion
  155.3 2.0 %divide_subtract_fusion = (f32[64,1024]{1,0:T(8,128)}, f32[64,1024]{1,0:T(8,128)S(1)}) fusion(f32[64,1024]{1,0:T(8,128)} %all-reduce.2.cloned.1.call-done, f32[64]{0:T(128)S(1)} %get-tuple-element.9, f32[8,1024]{1,0:T(8,128)S(1)} %convolution_divide_fusion, s32[64]{0:T(128)S(1)} %copy-done.1), kind=kOutput, calls=%fused_computation.26 | convolution fusion | flops 6423040 | bytes 819712 | tf_op jit(solution)/shard_map/dot_general | solution.py:97
  157.2 2.1 %fusion.19 = bf16[128,1024]{1,0:T(8,128)(2,1)} fusion(f32[64,1024]{1,0:T(8,128)S(1)} %get-tuple-element.16, bf16[128,1024]{1,0:T(8,128)(2,1)} %reduce-scatter.2.cloned.1.call-done, s32[64]{0:T(128)S(1)} %reduce, s32[64]{0:T(128)S(1)} %get-tuple-element.10, s32[128]{0:T(128)S(1)} %get-tuple-element.18), kind=kOutput, calls=%fused_computation.18 | convolution fusion | flops 101081088 | bytes 787456 | tf_op jit(solution)/shard_map/dot_general | solution.py:98
  (47 shorter events, 1.0 us)
Async XLA Ops:
  7.2 72.0 %reduce-scatter.2.cloned.1.call-start = ((), (), s32[]{:S(2)}) async-start(), calls=%async_computation.1 | async-start | bytes 1310720 | tf_op jit(solution)/shard_map/reduce_scatter | solution.py:81
  9.1 21.2 %collective-permute-start = (bf16[128,512]{0,1:T(8,128)(2,1)S(1)}, bf16[128,512]{0,1:T(8,128)(2,1)S(1)}, u32[]{:S(2)}, u32[]{:S(2)}) collective-permute-start(bf16[128,512]{0,1:T(8,128)(2,1)S(1)} %pad_maximum_fusion), channel_id=1, source_target_pairs={{0,4},{4,8},{8,12},{12,16},{16,20},{20,24},{24,28},{1,5},{5,9},{9,... | collective-permute-start | bytes 393224 | tf_op jit(solution)/shard_map/ppermute | solution.py:13
  14.0 17.6 %collective-permute-start.1 = (bf16[128,512]{0,1:T(8,128)(2,1)S(1)}, bf16[128,512]{0,1:T(8,128)(2,1)S(1)}, u32[]{:S(2)}, u32[]{:S(2)}) collective-permute-start(bf16[128,512]{0,1:T(8,128)(2,1)S(1)} %pad_maximum_fusion), channel_id=1, source_target_pairs={{4,0},{8,4},{12,8},{16,12},{20,16},{24,20},{28,24},{5,1},{9,5},{13... | collective-permute-start | bytes 393224 | tf_op jit(solution)/shard_map/ppermute | solution.py:13
  15.3 23.7 %collective-permute-start.2 = (bf16[128,512]{0,1:T(8,128)(2,1)S(1)}, bf16[128,512]{0,1:T(8,128)(2,1)S(1)}, u32[]{:S(2)}, u32[]{:S(2)}) collective-permute-start(bf16[128,512]{0,1:T(8,128)(2,1)S(1)} %pad_maximum_fusion), channel_id=1, source_target_pairs={{0,8},{4,12},{8,16},{12,20},{16,24},{20,28},{1,9},{5,13},{9,17},{1... | collective-permute-start | bytes 393224 | tf_op jit(solution)/shard_map/ppermute | solution.py:13
  20.8 19.5 %collective-permute-start.3 = (bf16[128,512]{0,1:T(8,128)(2,1)S(1)}, bf16[128,512]{0,1:T(8,128)(2,1)S(1)}, u32[]{:S(2)}, u32[]{:S(2)}) collective-permute-start(bf16[128,512]{0,1:T(8,128)(2,1)S(1)} %pad_maximum_fusion), channel_id=1, source_target_pairs={{8,0},{12,4},{16,8},{20,12},{24,16},{28,20},{9,1},{13,5},{17,9},{2... | collective-permute-start | bytes 393224 | tf_op jit(solution)/shard_map/ppermute | solution.py:13
  22.1 18.3 %collective-permute-start.4 = (bf16[128,512]{0,1:T(8,128)(2,1)S(1)}, bf16[128,512]{0,1:T(8,128)(2,1)S(1)}, u32[]{:S(2)}, u32[]{:S(2)}) collective-permute-start(bf16[128,512]{0,1:T(8,128)(2,1)S(1)} %pad_maximum_fusion), channel_id=1, source_target_pairs={{0,12},{4,16},{8,20},{12,24},{16,28},{1,13},{5,17},{9,21},{13,25},... | collective-permute-start | bytes 393224 | tf_op jit(solution)/shard_map/ppermute | solution.py:13
  30.3 10.2 %collective-permute-start.5 = (bf16[128,512]{0,1:T(8,128)(2,1)S(1)}, bf16[128,512]{0,1:T(8,128)(2,1)S(1)}, u32[]{:S(2)}, u32[]{:S(2)}) collective-permute-start(bf16[128,512]{0,1:T(8,128)(2,1)S(1)} %pad_maximum_fusion), channel_id=1, source_target_pairs={{12,0},{16,4},{20,8},{24,12},{28,16},{13,1},{17,5},{21,9},{25,13},... | collective-permute-start | bytes 393224 | tf_op jit(solution)/shard_map/ppermute | solution.py:13
  31.7 9.8 %collective-permute-start.6 = (bf16[128,512]{0,1:T(8,128)(2,1)S(1)}, bf16[128,512]{0,1:T(8,128)(2,1)S(1)}, u32[]{:S(2)}, u32[]{:S(2)}) collective-permute-start(bf16[128,512]{0,1:T(8,128)(2,1)S(1)} %pad_maximum_fusion), channel_id=1, source_target_pairs={{0,16},{4,20},{8,24},{12,28},{1,17},{5,21},{9,25},{13,29},{2,18},{... | collective-permute-start | bytes 393224 | tf_op jit(solution)/shard_map/ppermute | solution.py:13
  39.0 9.2 %collective-permute-start.7 = (bf16[128,512]{0,1:T(8,128)(2,1)S(1)}, bf16[128,512]{0,1:T(8,128)(2,1)S(1)}, u32[]{:S(2)}, u32[]{:S(2)}) collective-permute-start(bf16[128,512]{0,1:T(8,128)(2,1)S(1)} %pad_maximum_fusion), channel_id=1, source_target_pairs={{16,0},{20,4},{24,8},{28,12},{17,1},{21,5},{25,9},{29,13},{18,2},{... | collective-permute-start | bytes 393224 | tf_op jit(solution)/shard_map/ppermute | solution.py:13
  50.0 4.0 %slice-start = ((s8[8388608]{0:T(1024)(128)(4,1)}), s8[4194304]{0:T(1024)(128)(4,1)S(1)}, s32[]{:S(2)}) async-start(s8[8388608]{0:T(1024)(128)(4,1)} %bitcast.77), calls=%async_computation.3 | async-start | bytes 8388608
  52.4 2.2 %slice-start.1 = ((s8[8388608]{0:T(1024)(128)(4,1)}), s8[4194304]{0:T(1024)(128)(4,1)S(1)}, s32[]{:S(2)}) async-start(s8[8388608]{0:T(1024)(128)(4,1)} %bitcast.77), calls=%async_computation.4 | async-start | bytes 8388608
  54.6 2.3 %copy-start = (s32[64]{0:T(128)S(1)}, s32[64]{0:T(128)}, u32[]{:S(2)}) copy-start(s32[64]{0:T(128)} %param.12) | copy-start | bytes 772
  54.6 26.6 %copy-start.1 = (s32[64]{0:T(128)S(1)}, s32[64]{0:T(128)}, u32[]{:S(2)}) copy-start(s32[64]{0:T(128)} %param.13) | copy-start | bytes 772
  56.9 97.2 %all-reduce.2.cloned.1.call-start = ((), (), s32[]{:S(2)}) async-start(), calls=%async_computation.2 | async-start | bytes 524288 | tf_op jit(solution)/shard_map/psum | solution.py:90
Sparse Core Ops, SparseCore 0:
  57.0 22.1 reduce-scatter.1
  83.5 70.5 all-reduce.1
where the time goes:
time: 167 us; the launch traced here: 166 us
  waiting for transfers between devices  102 us (61%)
  starting transfers between devices  27.6 us (17%)
  between operations  14.4 us (9%)
  matrix products  13.1 us (8%)
  local copies, waits for them, and re-layouts  5.74 us (3%)
  other arithmetic  2.95 us (2%)
    psum x1, waiting for transfers between devices, on_device(): span_sum = lax.psum(span_part, 'seq')  72.8 us
    ppermute x8, starting transfers between devices, shifted(): return lax.ppermute(block, axis, route)  27.5 us
    reduce_scatter x1, waiting for transfers between devices, on_device(): lax.psum_scatter(partial_sums.astype(jnp.bfloat16), 'head', scatter_dimen...  22 us
    ppermute x8, waiting for transfers between devices, shifted(): return lax.ppermute(block, axis, route)  7.62 us
  transfers between devices with their start and end apart: 10, of which 4 were waited for; matrix products, arithmetic and copies ran while one was open for 2% of the time, Pallas kernels for 0%

commit v1 on v0

v1 whole, which is shorter than its diff:
```python
import functools

import jax
import jax.numpy as jnp
from jax import lax
from jax.experimental import pallas as pl
from jax.experimental.pallas import tpu as pltpu
from jax.sharding import PartitionSpec as P

HD = 128
NEG = -1e30
LOG2E = 1.4426950408889634


def remote(src, dst, send, recv, device):
    return pltpu.make_async_remote_copy(
        src_ref=src,
        dst_ref=dst,
        send_sem=send,
        recv_sem=recv,
        device_id=device,
        device_id_type=pl.DeviceIdType.MESH,
    )


def each(low, high, body):
    if high - low <= 8:
        for i in range(low, high):
            body(i)
    else:

        def step(i, carry):
            body(i)
            return carry

        lax.fori_loop(low, high, step, 0)


def pack(x):
    half = x.shape[1] // 2
    return jnp.concatenate([x[:, :half], x[:, half:]], axis=0)


def unpack(x):
    rows = x.shape[0] // 2
    return jnp.concatenate([x[:rows], x[rows:]], axis=1)


def dot(a, b, dims=((1,), (0,))):
    return lax.dot_general(a, b, (dims, ((), ())), preferred_element_type=jnp.float32)


def kernel(
    n, heads, reach, owners,
    q_ref, k_ref, v_ref, win_ref, len_ref, lang_ref, w_ref,
    cent_ref, pool_ref,
    kbuf, vbuf, qs, m_s, l_s, acc, attn, wbuf, pout, pin, xout, xin, toks,
    sp_out, sp_in, hs_out, hs_in, sf, hot_t, hot, same_s, cnt_s, len_s,
    kv_send, kv_recv, w_sem, p_send, p_recv, x_send, x_recv,
    s1_send, s1_recv, h_send, h_recv, s2_send, s2_recv,
):
    p = lax.axis_index("seq")
    hd_me = lax.axis_index("head")
    nx = heads // 2
    x, c = hd_me // 2, hd_me % 2
    tok = q_ref.shape[0]
    kv_heads = k_ref.shape[1] // HD
    group = q_ref.shape[1] // k_ref.shape[1]
    lanes = group * tok
    segs = len_ref.shape[1]
    radius = reach // 2
    pair, par = p // 2, p % 2
    chunks, jc = wbuf.shape[2], wbuf.shape[4]
    cols = chunks * jc
    stride = n // owners
    rows = segs // owners

    barrier = pltpu.get_barrier_semaphore()

    def greet_seq(i):
        pl.semaphore_signal(
            barrier, inc=1, device_id={"seq": (p + i) % n}, device_id_type=pl.DeviceIdType.MESH
        )

    each(1, n, greet_seq)
    for i in range(1, heads):
        pl.semaphore_signal(
            barrier,
            inc=1,
            device_id={"head": (hd_me + i) % heads},
            device_id_type=pl.DeviceIdType.MESH,
        )

    def w_copy(k, cc, j):
        side = c if cc else 1 - c
        off = (((x + k) % nx) * 2 + side) * cols + j * jc
        return pltpu.make_async_copy(
            w_ref.at[:, pl.ds(pl.multiple_of(off, 128), jc)], wbuf.at[k, cc, j], w_sem.at[k, cc, j]
        )

    x_order = list(range(1, nx)) + [0]
    pl.semaphore_wait(barrier, n - 1 + heads - 1)

    offsets = [s * d for d in range(1, reach + 1) for s in (1, -1)]

    def kv_copy(i, o, which):
        d = p + o
        r = pair - d // 2 + radius
        src, buf = ((k_ref, kbuf), (v_ref, vbuf))[which]
        return remote(
            src, buf.at[r, par], kv_send.at[i, which], kv_recv.at[r, par, which], {"seq": d}
        )

    for i, o in enumerate(offsets):

        @pl.when((p + o >= 0) & (p + o < n))
        def _():
            kv_copy(i, o, 0).start()
            kv_copy(i, o, 1).start()

    for k in x_order:
        for cc in range(2):
            for j in range(chunks):
                w_copy(k, cc, j).start()

    kbuf[radius, par] = k_ref[...]
    vbuf[radius, par] = v_ref[...]
    for g in range(kv_heads):
        for h in range(group):
            at = (g * group + h) * HD
            qs[g, h * tok : (h + 1) * tok, :] = q_ref[:, at : at + HD]

    i0 = lax.broadcasted_iota(jnp.int32, (segs, segs), 0)
    i1 = lax.broadcasted_iota(jnp.int32, (segs, segs), 1)
    len_row = len_ref[...].astype(jnp.float32)
    lang_row = lang_ref[...].astype(jnp.float32)
    len_b = jnp.broadcast_to(len_row, (segs, segs))
    lang_b = jnp.broadcast_to(lang_row, (segs, segs))
    ends_col = jnp.sum(jnp.where(i1 <= i0, len_b, 0.0), axis=1, keepdims=True)
    len_col = jnp.sum(jnp.where(i1 == i0, len_b, 0.0), axis=1, keepdims=True)
    lang_col = jnp.sum(jnp.where(i1 == i0, lang_b, 0.0), axis=1, keepdims=True)
    len_cb = jnp.broadcast_to(len_col, (segs, segs))
    ends_row = jnp.sum(jnp.where(i0 <= i1, len_cb, 0.0), axis=0, keepdims=True)
    same = lang_b == jnp.broadcast_to(lang_col, (segs, segs))
    cnt_s[...] = jnp.maximum(jnp.sum(jnp.where(same, len_b, 0.0), axis=1, keepdims=True), 1.0)
    len_s[...] = len_col
    same_s[...] = jnp.where(same, 1.0, 0.0).astype(jnp.bfloat16)
    pos_t = (lax.broadcasted_iota(jnp.int32, (segs, tok), 1) + p * tok).astype(jnp.float32)
    in_t = (pos_t >= ends_col - len_col) & (pos_t < ends_col)
    hot_t[...] = jnp.where(in_t, 1.0, 0.0).astype(jnp.bfloat16)
    pos = (lax.broadcasted_iota(jnp.int32, (tok, segs), 0) + p * tok).astype(jnp.float32)
    in_s = (pos >= ends_row - len_row) & (pos < ends_row)
    hot[...] = jnp.where(in_s, 1.0, 0.0).astype(jnp.bfloat16)

    win_rows = []
    for g in range(kv_heads):
        parts = [
            jnp.full((1, tok), win_ref[hd_me * kv_heads * group + g * group + h], jnp.int32)
            for h in range(group)
        ]
        win_rows.append(jnp.concatenate(parts, axis=1))

    m_s[...] = jnp.full(m_s.shape, NEG, jnp.float32)
    l_s[...] = jnp.zeros(l_s.shape, jnp.float32)
    acc[...] = jnp.zeros(acc.shape, jnp.float32)
    scale = HD**-0.5 * LOG2E

    def absorb(t, carry):
        away = (t + 1) // 2
        there = jnp.where(t % 2 == 1, -away, away)
        r = radius + there

        @pl.when((pair + there >= 0) & (pair + there < n // 2))
        def _():
            for b in range(2):
                block = 2 * (pair + there) + b
                gap = jnp.abs(block - p)

                @pl.when((gap > 0) & (gap <= reach))
                def _():
                    for which, buf in enumerate((kbuf, vbuf)):
                        remote(
                            buf.at[r, b],
                            buf.at[r, b],
                            kv_send.at[0, which],
                            kv_recv.at[r, b, which],
                            {"seq": block},
                        ).wait_recv()

                @pl.when(gap > reach)
                def _():
                    kbuf[r, b] = jnp.zeros(kbuf.shape[2:], kbuf.dtype)
                    vbuf[r, b] = jnp.zeros(vbuf.shape[2:], vbuf.dtype)

            keys = kbuf[r].reshape(2 * tok, kv_heads * HD)
            vals = vbuf[r].reshape(2 * tok, kv_heads * HD)
            key_pos = lax.broadcasted_iota(jnp.int32, (2 * tok, tok), 0)
            query_pos = lax.broadcasted_iota(jnp.int32, (2 * tok, tok), 1)
            dist = jnp.abs(key_pos - query_pos + (2 * (pair + there) - p) * tok)
            dist = jnp.concatenate([dist] * group, axis=1)
            for g in range(kv_heads):
                kb = keys[:, g * HD : (g + 1) * HD]
                vb = vals[:, g * HD : (g + 1) * HD]
                s = dot(kb, qs[g], ((1,), (1,)))
                s = jnp.where(dist <= win_rows[g], s, NEG)
                m_old = m_s[g]
                m_new = jnp.maximum(m_old, jnp.max(s, axis=0, keepdims=True))
                alpha = jnp.exp2((m_old - m_new) * scale)
                prob = jnp.exp2((s - m_new) * scale)
                l_s[g] = l_s[g] * alpha + jnp.sum(prob, axis=0, keepdims=True)
                acc[g] = acc[g] * alpha + dot(vb, prob.astype(jnp.bfloat16), ((0,), (0,)))
                m_s[g] = m_new

        return carry

    lax.fori_loop(0, 2 * radius + 1, absorb, 0)

    for g in range(kv_heads):
        a = acc[g] / l_s[g]
        for h in range(group):
            at = (g * group + h) * HD
            attn[:, at : at + HD] = a[:, h * tok : (h + 1) * tok].T.astype(jnp.bfloat16)

    summed = dot(hot_t[...], attn[...])
    for o in range(owners):
        sp_out[o] = pack(summed[o * rows : (o + 1) * rows]).astype(jnp.bfloat16)
    mine = p // stride

    def is_owner(d, body):
        if stride == 1:
            body()
        else:
            pl.when(d % stride == 0)(body)

    def s1_copy(i):
        d = (p + i) % n
        return remote(
            sp_out.at[d // stride], sp_in.at[p], s1_send.at[i], s1_recv.at[p], {"seq": d}
        )

    each(1, n, lambda i: is_owner((p + i) % n, lambda: s1_copy(i).start()))

    partner = x * 2 + 1 - c

    def p_copy(k, j):
        return remote(
            pout.at[k, j], pin.at[k, j], p_send.at[k, j], p_recv.at[k, j], {"head": partner}
        )

    def x_copy(k, j):
        to = ((x + k) % nx) * 2 + c
        return remote(xout.at[k, j], xin.at[k, j], x_send.at[k, j], x_recv.at[k, j], {"head": to})

    for k in x_order:

        def for_partner(j, carry):
            w_copy(k, 0, j).wait()
            pout[k, j] = dot(attn[...], wbuf[k, 0, j]).astype(jnp.bfloat16)
            p_copy(k, j).start()
            return carry

        lax.fori_loop(0, chunks, for_partner, 0)

        def for_me(j, carry):
            w_copy(k, 1, j).wait()
            part = dot(attn[...], wbuf[k, 1, j])
            p_copy(k, j).wait_recv()
            part = part + pin[k, j].astype(jnp.float32)
            if k:
                xout[k, j] = part.astype(jnp.bfloat16)
                x_copy(k, j).start()
            else:
                toks[j] = part
            return carry

        lax.fori_loop(0, chunks, for_me, 0)

    def h_copy(k, cc):
        side = c if cc else 1 - c
        to = ((x + k) % nx) * 2 + side
        return remote(
            hs_out.at[k, cc], hs_in.at[k, cc], h_send.at[k, cc], h_recv.at[k, cc], {"head": to}
        )

    def s2_copy(i):
        return remote(sf.at[mine], sf.at[mine], s2_send.at[i], s2_recv.at[mine], {"seq": (p + i) % n})

    others = [(k, cc) for k in x_order for cc in range(2) if k or not cc]

    def own_spans():
        def take(i):
            d = (p + i) % n
            remote(
                sp_in.at[d], sp_in.at[d], s1_send.at[i], s1_recv.at[d], {"seq": d}
            ).wait_recv()

        each(1, n, take)
        sp_in[p] = sp_out[mine]
        total = unpack(jnp.sum(sp_in[...].astype(jnp.float32), axis=0))
        high = total.astype(jnp.bfloat16)
        low = (total - high.astype(jnp.float32)).astype(jnp.bfloat16)
        both = jnp.concatenate([high, low], axis=0)

        def through(k, cc):
            made = [dot(both, wbuf[k, cc, j]) for j in range(chunks)]
            return jnp.concatenate([y[:rows] + y[rows:] for y in made], axis=1)

        for k, cc in others:
            hs_out[k, cc] = pack(through(k, cc)).astype(jnp.bfloat16)
            h_copy(k, cc).start()
        result = pack(through(0, 1))
        for k, cc in others:
            h_copy(k, cc).wait_recv()
            result = result + hs_in[k, cc].astype(jnp.float32)
        sf[mine] = result.astype(jnp.bfloat16)
        each(1, n, lambda i: s2_copy(i).start())

    is_owner(p, own_spans)

    for j in range(chunks):
        for k in range(1, nx):
            x_copy(k, j).wait_recv()
            toks[j] = toks[j] + xin[k, j].astype(jnp.float32)

    def take_spans(i):
        d = (p + i) % n

        def take():
            o = d // stride
            remote(sf.at[o], sf.at[o], s2_send.at[i], s2_recv.at[o], {"seq": d}).wait_recv()

        is_owner(d, take)

    each(1, n, take_spans)

    spans = jnp.concatenate([unpack(sf[o]) for o in range(owners)], axis=0)
    center = dot(same_s[...], spans) / cnt_s[...]
    pool_ref[...] = spans.astype(jnp.float32) / len_s[...] - center
    high = center.astype(jnp.bfloat16)
    low = (center - high.astype(jnp.float32)).astype(jnp.bfloat16)
    moved = dot(hot[...], high) + dot(hot[...], low)
    for j in range(chunks):
        at = slice(j * jc, (j + 1) * jc)
        cent_ref[:, at] = (toks[j] - moved[:, at]).astype(jnp.bfloat16)

    for i, o in enumerate(offsets):

        @pl.when((p + o >= 0) & (p + o < n))
        def _():
            kv_copy(i, o, 0).wait_send()
            kv_copy(i, o, 1).wait_send()

    each(1, n, lambda i: is_owner((p + i) % n, lambda: s1_copy(i).wait_send()))
    for k in range(nx):
        for j in range(chunks):
            p_copy(k, j).wait_send()
            if k:
                x_copy(k, j).wait_send()

    def own_sends():
        for k, cc in others:
            h_copy(k, cc).wait_send()
        each(1, n, lambda i: s2_copy(i).wait_send())

    is_owner(p, own_sends)


def on_device(n, heads, queries, keys, values, out_weight, windows, seg_lengths, lang_ids):
    tok, q_cols = queries.shape
    kv_cols = keys.shape[1]
    kv_heads, group = kv_cols // HD, q_cols // kv_cols
    depth, width = out_weight.shape
    cols = width // heads
    segs = seg_lengths.shape[0]
    reach = min(16, n // 2)
    radius = reach // 2
    owners = min(n, segs // 8)
    rows = segs // owners
    nx = heads // 2
    chunks = 4
    jc = cols // chunks
    lanes = group * tok
    slots = 2 * radius + 1
    bf, f32 = jnp.bfloat16, jnp.float32
    packed = (2 * rows, cols // 2)
    packed_in = (2 * rows, q_cols // 2)
    dma = pltpu.SemaphoreType.DMA
    vmem = pl.BlockSpec(memory_space=pltpu.VMEM)
    return pl.pallas_call(
        functools.partial(kernel, n, heads, reach, owners),
        out_shape=(
            jax.ShapeDtypeStruct((tok, cols), bf),
            jax.ShapeDtypeStruct((segs, cols), f32),
        ),
        in_specs=[
            vmem,
            vmem,
            vmem,
            pl.BlockSpec(memory_space=pltpu.SMEM),
            vmem,
            vmem,
            pl.BlockSpec(memory_space=pl.ANY),
        ],
        out_specs=(vmem, vmem),
        scratch_shapes=[
            pltpu.VMEM((slots, 2, tok, kv_cols), bf),
            pltpu.VMEM((slots, 2, tok, kv_cols), bf),
            pltpu.VMEM((kv_heads, lanes, HD), bf),
            pltpu.VMEM((kv_heads, 1, lanes), f32),
            pltpu.VMEM((kv_heads, 1, lanes), f32),
            pltpu.VMEM((kv_heads, HD, lanes), f32),
            pltpu.VMEM((tok, q_cols), bf),
            pltpu.VMEM((nx, 2, chunks, depth, jc), bf),
            pltpu.VMEM((nx, chunks, tok, jc), bf),
            pltpu.VMEM((nx, chunks, tok, jc), bf),
            pltpu.VMEM((nx, chunks, tok, jc), bf),
            pltpu.VMEM((nx, chunks, tok, jc), bf),
            pltpu.VMEM((chunks, tok, jc), f32),
            pltpu.VMEM((owners,) + packed_in, bf),
            pltpu.VMEM((n,) + packed_in, bf),
            pltpu.VMEM((nx, 2) + packed, bf),
            pltpu.VMEM((nx, 2) + packed, bf),
            pltpu.VMEM((owners,) + packed, bf),
            pltpu.VMEM((segs, tok), bf),
            pltpu.VMEM((tok, segs), bf),
            pltpu.VMEM((segs, segs), bf),
            pltpu.VMEM((segs, 1), f32),
            pltpu.VMEM((segs, 1), f32),
            dma((2 * reach, 2)),
            dma((slots, 2, 2)),
            dma((nx, 2, chunks)),
            dma((nx, chunks)),
            dma((nx, chunks)),
            dma((nx, chunks)),
            dma((nx, chunks)),
            dma((n,)),
            dma((n,)),
            dma((nx, 2)),
            dma((nx, 2)),
            dma((n,)),
            dma((owners,)),
        ],
        compiler_params=pltpu.CompilerParams(
            collective_id=0, has_side_effects=True, vmem_limit_bytes=40 * 2**20
        ),
        cost_estimate=pl.CostEstimate(
            flops=2 * tok * depth * width, bytes_accessed=2 * depth * width, transcendentals=0
        ),
    )(
        queries,
        keys,
        values,
        windows,
        seg_lengths.reshape(1, segs),
        lang_ids.reshape(1, segs),
        out_weight,
    )


def solution(mesh):
    in_specs = (
        P("seq", "head"),
        P("seq", "head"),
        P("seq", "head"),
        P("head", None),
        P(),
        P(),
        P(),
    )
    out_specs = (P("seq", "head"), P(None, "head"))
    return jax.shard_map(
        functools.partial(on_device, mesh.shape["seq"], mesh.shape["head"]),
        mesh=mesh,
        in_specs=in_specs,
        out_specs=out_specs,
        check_vma=False,
    )
```

time: 167 us -> 52.2 us (0.31)
  waiting for transfers between devices: 102 us -> 0 us
  Pallas kernels: 0 us -> 41.9 us
  starting transfers between devices: 27.6 us -> 0 us
  between operations: 14.4 us -> 0.66 us
  matrix products: 13.1 us -> 0 us
  local copies, waits for them, and re-layouts: 5.74 us -> 9.37 us
  other arithmetic: 2.95 us -> 0 us
    psum x1 -> x0, waiting for transfers between devices: 72.8 us -> none  [on_device(): span_sum = lax.psum(span_part, 'seq')]
    pallas_call x0 -> x1, Pallas kernels: none -> 41.9 us  [on_device(): pl.pallas_call(functools.partial(kernel, n, heads, reach, owners), out_sh...]
    ppermute x8 -> x0, starting transfers between devices: 27.5 us -> none  [shifted(): return lax.ppermute(block, axis, route)]
    reduce_scatter x1 -> x0, waiting for transfers between devices: 22 us -> none  [on_device(): lax.psum_scatter(partial_sums.astype(jnp.bfloat16), 'head', scatter_dimen...]
    dot_general x9 -> x0, matrix products: 13.1 us -> none  [the longest x1 2.26 us: on_device(): partial_sums = jnp.dot(attn, out_weight, preferred_element_type=jnp.float32)]
    ppermute x8 -> x0, waiting for transfers between devices: 7.62 us -> none  [shifted(): return lax.ppermute(block, axis, route)]
    unnamed x16, local copies, waits for them, and re-layouts: 1.79 us -> 9.37 us
    reshape x3 -> x0, local copies, waits for them, and re-layouts: 2.93 us -> none  [the longest x1 1.12 us: on_device(): query_grid = queries.reshape(tok, kv_heads, group, HD)]
  transfers between devices with their start and end apart: 10 -> 0, of which waited for: 4 -> 0; matrix products, arithmetic and copies ran while one was open for 2% -> 0% of each run, Pallas kernels for 0% -> 0%
where the time goes in v1:
time: 52.2 us; the launch traced here: 51.9 us
  Pallas kernels  41.9 us (80%)
  local copies, waits for them, and re-layouts  9.37 us (18%)
  between operations  0.66 us (1%)
    pallas_call x1, Pallas kernels, on_device(): pl.pallas_call(functools.partial(kernel, n, heads, reach, owners), out_sh...  41.9 us
    unnamed x16, local copies, waits for them, and re-layouts  9.37 us

profile of v1, /device:TPU:0, one launch (start us, length us, event | category | flops | bytes accessed | tf_op | source)
XLA Modules:
  0.0 51.9 jit_solution(11926602697103878448)
XLA Ops:
  0.6 0.0 copy-start
  0.6 3.4 %copy-done = bf16[1024,4096]{1,0:T(8,128)(2,1)S(1)} copy-done((bf16[1024,4096]{1,0:T(8,128)(2,1)S(1)}, bf16[1024,4096]{1,0:T(8,128)(2,1)}, u32[]{:S(2)}) %copy-start) | copy-done | bytes 8388632
  4.0 0.0 copy-start.1
  4.0 0.9 %copy-done.1 = bf16[128,1024]{1,0:T(8,128)(2,1)S(1)} copy-done((bf16[128,1024]{1,0:T(8,128)(2,1)S(1)}, bf16[128,1024]{1,0:T(8,128)(2,1)}, u32[]{:S(2)}) %copy-start.1) | copy-done | bytes 262168
  5.0 0.0 copy-start.2
  5.0 0.8 %copy-done.2 = bf16[128,256]{1,0:T(8,128)(2,1)S(1)} copy-done((bf16[128,256]{1,0:T(8,128)(2,1)S(1)}, bf16[128,256]{1,0:T(8,128)(2,1)}, u32[]{:S(2)}) %copy-start.2) | copy-done | bytes 65560
  5.8 0.0 copy-start.3
  5.8 0.8 %copy-done.3 = bf16[128,256]{1,0:T(8,128)(2,1)S(1)} copy-done((bf16[128,256]{1,0:T(8,128)(2,1)S(1)}, bf16[128,256]{1,0:T(8,128)(2,1)}, u32[]{:S(2)}) %copy-start.3) | copy-done | bytes 65560
  6.6 0.0 copy-start.4
  6.6 0.7 %copy-done.4 = s32[32]{0:T(128)S(1)} copy-done((s32[32]{0:T(128)S(1)}, s32[32]{0:T(128)}, u32[]{:S(2)}) %copy-start.4) | copy-done | bytes 152
  7.3 0.0 copy-start.5
  7.3 0.7 %copy-done.5 = s32[64]{0:T(128)S(1)} copy-done((s32[64]{0:T(128)S(1)}, s32[64]{0:T(128)}, u32[]{:S(2)}) %copy-start.5) | copy-done | bytes 280
  8.0 0.0 copy-start.6
  8.0 0.7 %copy-done.6 = s32[64]{0:T(128)S(1)} copy-done((s32[64]{0:T(128)S(1)}, s32[64]{0:T(128)}, u32[]{:S(2)}) %copy-start.6) | copy-done | bytes 280
  8.6 41.9 %shard_map.86 = (bf16[128,1024]{1,0:T(8,128)(2,1)S(1)}, f32[64,1024]{1,0:T(8,128)S(1)}) custom-call(bf16[128,1024]{1,0:T(8,128)(2,1)S(1)} %copy-done.1, bf16[128,256]{1,0:T(8,128)(2,1)S(1)} %copy-done.2, bf16[128,256]{1,0:T(8,128)(2,1)S(1)} %copy-done.3, s32[32]{0:T(128)S(1)} %copy-done.4, s32[1,64]{1,0:T(1,128)S(1)} %bitcast.2, s32[1,64]{1,0:T(1,128)S(1)} %bitcast.3, ...), custom_call_target="tpu_custom_call" | custom-call | flops 1073741824 | bytes 8388608 | tf_op jit(solution)/shard_map/pallas_call | solution.py:389
  50.5 0.7 %copy.11 = bf16[128,1024]{1,0:T(8,128)(2,1)} copy(bf16[128,1024]{1,0:T(8,128)(2,1)S(1)} %get-tuple-element.4) | data formatting | bytes 524288
  51.2 0.7 %copy.12 = f32[64,1024]{1,0:T(8,128)} copy(f32[64,1024]{1,0:T(8,128)S(1)} %get-tuple-element.5) | data formatting | bytes 524288
Async XLA Ops:
  0.6 3.4 %copy-start = (bf16[1024,4096]{1,0:T(8,128)(2,1)S(1)}, bf16[1024,4096]{1,0:T(8,128)(2,1)}, u32[]{:S(2)}) copy-start(bf16[1024,4096]{1,0:T(8,128)(2,1)} %w_ref.1) | copy-start | bytes 25165828
  4.0 0.9 %copy-start.1 = (bf16[128,1024]{1,0:T(8,128)(2,1)S(1)}, bf16[128,1024]{1,0:T(8,128)(2,1)}, u32[]{:S(2)}) copy-start(bf16[128,1024]{1,0:T(8,128)(2,1)} %q_ref.1) | copy-start | bytes 786436
  5.0 0.8 %copy-start.2 = (bf16[128,256]{1,0:T(8,128)(2,1)S(1)}, bf16[128,256]{1,0:T(8,128)(2,1)}, u32[]{:S(2)}) copy-start(bf16[128,256]{1,0:T(8,128)(2,1)} %k_ref.1) | copy-start | bytes 196612
  5.8 0.8 %copy-start.3 = (bf16[128,256]{1,0:T(8,128)(2,1)S(1)}, bf16[128,256]{1,0:T(8,128)(2,1)}, u32[]{:S(2)}) copy-start(bf16[128,256]{1,0:T(8,128)(2,1)} %v_ref.1) | copy-start | bytes 196612
  6.6 0.7 %copy-start.4 = (s32[32]{0:T(128)S(1)}, s32[32]{0:T(128)}, u32[]{:S(2)}) copy-start(s32[32]{0:T(128)} %win_ref.1) | copy-start | bytes 388
  7.3 0.7 %copy-start.5 = (s32[64]{0:T(128)S(1)}, s32[64]{0:T(128)}, u32[]{:S(2)}) copy-start(s32[64]{0:T(128)} %param.12) | copy-start | bytes 772
  8.0 0.7 %copy-start.6 = (s32[64]{0:T(128)S(1)}, s32[64]{0:T(128)}, u32[]{:S(2)}) copy-start(s32[64]{0:T(128)} %param.13) | copy-start | bytes 772

commit v2 on v1

--- a/solution.py
+++ b/solution.py
@@ -52,21 +52,20 @@
 
 def kernel(
     n, heads, reach, owners,
-    q_ref, k_ref, v_ref, win_ref, len_ref, lang_ref, w_ref,
+    q_hbm, k_ref, v_ref, win_hbm, len_hbm, lang_hbm, w_ref,
     cent_ref, pool_ref,
-    kbuf, vbuf, qs, m_s, l_s, acc, attn, wbuf, pout, pin, xout, xin, toks,
+    win_ref, len_ref, lang_ref, kbuf, vbuf, qs, m_s, l_s, acc, attn, wbuf, pout, pin, xout, xin, toks,
     sp_out, sp_in, hs_out, hs_in, sf, hot_t, hot, same_s, cnt_s, len_s,
     kv_send, kv_recv, w_sem, p_send, p_recv, x_send, x_recv,
-    s1_send, s1_recv, h_send, h_recv, s2_send, s2_recv,
+    s1_send, s1_recv, h_send, h_recv, s2_send, s2_recv, in_sem, q_sem,
 ):
     p = lax.axis_index("seq")
     hd_me = lax.axis_index("head")
     nx = heads // 2
     x, c = hd_me // 2, hd_me % 2
-    tok = q_ref.shape[0]
+    tok = q_hbm.shape[0]
     kv_heads = k_ref.shape[1] // HD
-    group = q_ref.shape[1] // k_ref.shape[1]
-    lanes = group * tok
+    group = q_hbm.shape[1] // k_ref.shape[1]
     segs = len_ref.shape[1]
     radius = reach // 2
     pair, par = p // 2, p % 2
@@ -99,6 +98,30 @@
         )
 
     x_order = list(range(1, nx)) + [0]
+    small = [
+        pltpu.make_async_copy(src, dst, in_sem.at[i])
+        for i, (src, dst) in enumerate(
+            (
+                (len_hbm, len_ref),
+                (lang_hbm, lang_ref),
+                (win_hbm, win_ref),
+                (k_ref, kbuf.at[radius, par]),
+                (v_ref, vbuf.at[radius, par]),
+            )
+        )
+    ]
+    for g in range(kv_heads):
+        for h in range(group):
+            at = (g * group + h) * HD
+            small.append(
+                pltpu.make_async_copy(
+                    q_hbm.at[:, at : at + HD],
+                    qs.at[g, h * tok : (h + 1) * tok, :],
+                    q_sem.at[g, h],
+                )
+            )
+    for copy in small:
+        copy.start()
     pl.semaphore_wait(barrier, n - 1 + heads - 1)
 
     offsets = [s * d for d in range(1, reach + 1) for s in (1, -1)]
@@ -123,12 +146,8 @@
             for j in range(chunks):
                 w_copy(k, cc, j).start()
 
-    kbuf[radius, par] = k_ref[...]
-    vbuf[radius, par] = v_ref[...]
-    for g in range(kv_heads):
-        for h in range(group):
-            at = (g * group + h) * HD
-            qs[g, h * tok : (h + 1) * tok, :] = q_ref[:, at : at + HD]
+    for copy in small:
+        copy.wait()
 
     i0 = lax.broadcasted_iota(jnp.int32, (segs, segs), 0)
     i1 = lax.broadcasted_iota(jnp.int32, (segs, segs), 1)
@@ -392,17 +411,12 @@
             jax.ShapeDtypeStruct((tok, cols), bf),
             jax.ShapeDtypeStruct((segs, cols), f32),
         ),
-        in_specs=[
-            vmem,
-            vmem,
-            vmem,
-            pl.BlockSpec(memory_space=pltpu.SMEM),
-            vmem,
-            vmem,
-            pl.BlockSpec(memory_space=pl.ANY),
-        ],
+        in_specs=[pl.BlockSpec(memory_space=pl.ANY)] * 7,
         out_specs=(vmem, vmem),
         scratch_shapes=[
+            pltpu.SMEM(windows.shape, jnp.int32),
+            pltpu.VMEM((1, segs), jnp.int32),
+            pltpu.VMEM((1, segs), jnp.int32),
             pltpu.VMEM((slots, 2, tok, kv_cols), bf),
             pltpu.VMEM((slots, 2, tok, kv_cols), bf),
             pltpu.VMEM((kv_heads, lanes, HD), bf),
@@ -439,9 +453,11 @@
             dma((nx, 2)),
             dma((n,)),
             dma((owners,)),
+            dma((5,)),
+            dma((kv_heads, group)),
         ],
         compiler_params=pltpu.CompilerParams(
-            collective_id=0, has_side_effects=True, vmem_limit_bytes=40 * 2**20
+            collective_id=0, has_side_effects=True, vmem_limit_bytes=57 * 2**20
         ),
         cost_estimate=pl.CostEstimate(
             flops=2 * tok * depth * width, bytes_accessed=2 * depth * width, transcendentals=0

time: 52.2 us -> 46.6 us (0.89)
  local copies, waits for them, and re-layouts: 9.37 us -> 3.34 us
    unnamed x16 -> x2, local copies, waits for them, and re-layouts: 9.37 us -> 3.34 us
    pallas_call x1, Pallas kernels: 41.9 us -> 42.4 us  [on_device(): pl.pallas_call(functools.partial(kernel, n, heads, reach, owners), out_sh...]
where the time goes in v2:
time: 46.6 us; the launch traced here: 46.4 us
  Pallas kernels  42.4 us (91%)
  local copies, waits for them, and re-layouts  3.34 us (7%)
  between operations  0.64 us (1%)
    pallas_call x1, Pallas kernels, on_device(): pl.pallas_call(functools.partial(kernel, n, heads, reach, owners), out_sh...  42.4 us
    unnamed x2, local copies, waits for them, and re-layouts  3.34 us

profile of v2, /device:TPU:0, one launch (start us, length us, event | category | flops | bytes accessed | tf_op | source)
XLA Modules:
  0.0 46.4 jit_solution(5013701618194814309)
XLA Ops:
  0.6 42.4 %shard_map.86 = (bf16[128,1024]{1,0:T(8,128)(2,1)}, f32[64,1024]{1,0:T(8,128)}) custom-call(bf16[128,1024]{1,0:T(8,128)(2,1)} %q_hbm.1, bf16[128,256]{1,0:T(8,128)(2,1)} %k_ref.1, bf16[128,256]{1,0:T(8,128)(2,1)} %v_ref.1, s32[32]{0:T(128)} %win_hbm.1, s32[1,64]{1,0:T(1,128)} %bitcast.2, s32[1,64]{1,0:T(1,128)} %bitcast.3, bf16[1024,4096]{1,0:T(8,128)(2,1)} %w_ref.1), custom_call_target="tpu_custom_call" | custom-call | flops 1073741824 | bytes 8388608 | tf_op jit(solution)/shard_map/pallas_call | solution.py:408
  43.1 1.7 %copy.11 = bf16[128,1024]{1,0:T(8,128)(2,1)} copy(bf16[128,1024]{1,0:T(8,128)(2,1)} %get-tuple-element.4) | data formatting | bytes 524288
  44.7 1.7 %copy.12 = f32[64,1024]{1,0:T(8,128)} copy(f32[64,1024]{1,0:T(8,128)} %get-tuple-element.5) | data formatting | bytes 524288
